TPU v7x, 256 devices: a whole 4x4x8 slice. The times are simulated.
256 devices in a mesh: row: 8 (over x, core), col: 32 (over z, y).
Axes of the slice: x: 4, y: 4, z: 8, core: 2. Of those that a mesh axis runs over, the one named last changes fastest.
Arguments:
- adj_trailing: bfloat16 [8192, 32768], P('row', 'col'), may hold values from -6 to 6
- panel_rows0: bfloat16 [8192, 512], P('row'), may hold values from -0.0625 to 0.0625
- panel_rows1: bfloat16 [8192, 512], P('row'), may hold values from -0.0625 to 0.0625
- panel_cols0: bfloat16 [32768, 512], P('col'), may hold values from -0.03125 to 0.03125
- panel_cols1: bfloat16 [32768, 512], P('col'), may hold values from -0.03125 to 0.03125
- inv_diag0: float32 [512, 512], replicated, as said below
- inv_diag1: float32 [512, 512], replicated, as said below
- cross_block: float32 [512, 512], replicated, may hold values from -0.25 to 0.25
- panel_adj0: bfloat16 [8192, 512], P(('row', 'col')), may hold values from -6 to 6
- panel_adj1: bfloat16 [8192, 512], P(('row', 'col')), may hold values from -6 to 6
Outputs:
- row_adj1: float32 [8192, 512], P(('row', 'col'))
- row_adj0: float32 [8192, 512], P(('row', 'col'))
- col_adj1: float32 [32768, 512], P('col')
- col_adj0: float32 [32768, 512], P('col')
- diag_adj1: float32 [512, 512], replicated
- diag_adj0: float32 [512, 512], replicated
Inputs may be any that keep to these rules, and one draw needn't show every extreme that they name: `inv_diag0`: lower triangular, with diagonal entries of 1 to 2. `inv_diag1`: lower triangular, with diagonal entries of 1 to 2.
All inputs are finite; a program needn't handle non-finite values.
Results may differ from a plain program's by a relative error of at most 0.0003.
Values sent between devices are 32-bit elements; how exact they have to be, the bound alone decides.
A program may use at most 128 MiB of HBM per device.

v0:
```python
import jax
import jax.numpy as jnp
from jax import lax
from jax.sharding import Mesh
from jax.sharding import PartitionSpec as P

COL = ("col_0", "col_1")
ROW = ("row_0", "row_1")
ROW_COL = ("row_0", "row_1", "col_0", "col_1")


def summed_rows(total, axes):
    for axis in axes:
        total = lax.psum_scatter(total, axis, scatter_dimension=0, tiled=True)
    return total


def in_blocks(shard, dim, length):
    dims = shard.shape
    tiles = shard.reshape(*dims[:dim], length, dims[dim] // length, *dims[dim + 1 :])
    return jnp.moveaxis(tiles, dim, 0)


def sum_at_owner(shard, axis, dim):
    length = lax.axis_size(axis)
    tiles = lax.all_to_all(in_blocks(shard, dim, length), axis, 0, 0, tiled=True)
    return jnp.sum(tiles, axis=0)


def sum_by_axis(shard, axes, dim):
    far, near = axes
    own = sum_at_owner(in_blocks(shard, dim, lax.axis_size(far)), near, dim + 1)
    return jnp.sum(lax.all_to_all(own, far, 0, 0, tiled=True), axis=0)


def padded_to(lines, length):
    spare = -len(lines) % length
    return jnp.pad(lines, [(0, spare)] + [(0, 0)] * (lines.ndim - 1))


def sent_to_all(shard, axis):
    copies = jnp.broadcast_to(shard, (lax.axis_size(axis), *shard.shape))
    return lax.all_to_all(copies, axis, split_axis=0, concat_axis=0, tiled=True)


def joined_along(tiles, dim):
    dims = list(tiles.shape[1:])
    dims[dim] *= tiles.shape[0]
    return jnp.moveaxis(tiles, 0, dim).reshape(dims)


def whole_of(shard, axes, dim):
    far, near = axes
    tiles = sent_to_all(sent_to_all(shard, far), near)
    return joined_along(tiles.swapaxes(0, 1).reshape(-1, *shard.shape), dim)


def nested_sum(shard, axes):
    own = sum_by_axis(padded_to(shard, lax.axis_size(axes[0]) * lax.axis_size(axes[1])), axes, 0)
    whole = whole_of(own, axes, 0)
    return whole[: len(shard)].reshape(shard.shape)


def packed_total(arrays, axis):
    line, at, outs = (jnp.concatenate([a.reshape(-1) for a in arrays]), 0, [])
    total = nested_sum(line, axis)
    for a in arrays:
        outs.append(total[at : at + a.size].reshape(a.shape))
        at += a.size
    return tuple(outs)


def trailing_term(adj_trailing, columns):
    return jnp.dot(adj_trailing, columns, preferred_element_type=jnp.float32)


def column_term(adj_trailing, rows):
    return -jnp.einsum("rc,rb->cb", adj_trailing, rows, preferred_element_type=jnp.float32)


def local(
    adj_trailing,
    panel_rows0,
    panel_rows1,
    panel_cols0,
    panel_cols1,
    inv_diag0,
    inv_diag1,
    cross_block,
    panel_adj0,
    panel_adj1,
):
    highest = lax.Precision.HIGHEST
    share = panel_adj1.shape[0]
    width = panel_cols1.shape[1]
    offset = lax.axis_index(COL) * share
    own_rows1 = lax.dynamic_slice_in_dim(panel_rows1, offset, share, 0).astype(jnp.float32)
    own_rows0 = lax.dynamic_slice_in_dim(panel_rows0, offset, share, 0).astype(jnp.float32)
    both_cols = jnp.concatenate((panel_cols1, panel_cols0), axis=1)
    trail = summed_rows(trailing_term(adj_trailing, both_cols), COL)
    trail1 = trail[:, :width]
    trail0 = trail[:, width:]
    both_rows = jnp.concatenate((panel_rows1, panel_rows0), axis=1)
    column_sum = lax.psum(column_term(adj_trailing, both_rows), ROW)
    col_adj1 = column_sum[:, :width]
    col_adj0 = column_sum[:, width:]
    bar1 = panel_adj1.astype(jnp.float32) - trail1
    row_adj1 = jnp.dot(bar1, inv_diag1, precision=highest)
    bar0 = (
        panel_adj0.astype(jnp.float32) - trail0 - jnp.dot(row_adj1, cross_block, precision=highest)
    )
    row_adj0 = jnp.dot(bar0, inv_diag0, precision=highest)
    gram1 = jnp.dot(bar1.T, own_rows1, precision=highest)
    gram0 = jnp.dot(bar0.T, own_rows0, precision=highest)
    local1 = jnp.dot(inv_diag1.T, gram1, precision=highest)
    local0 = jnp.dot(inv_diag0.T, gram0, precision=highest)
    summed1, summed0 = packed_total((local1, local0), (("row_0", "row_1", "col_0"), "col_1"))
    diag_adj1 = -jnp.tril(summed1)
    diag_adj0 = -jnp.tril(summed0)
    return (row_adj1, row_adj0, col_adj1, col_adj0, diag_adj1, diag_adj0)


def solution(mesh):
    finer = Mesh(mesh.devices.reshape(4, 2, 8, 4), ("row_0", "row_1", "col_0", "col_1"))
    in_specs = (
        P(ROW, COL),
        P(ROW, None),
        P(ROW, None),
        P(COL, None),
        P(COL, None),
        P(),
        P(),
        P(),
        P(ROW_COL, None),
        P(ROW_COL, None),
    )
    out_specs = (P(ROW_COL, None), P(ROW_COL, None), P(COL, None), P(COL, None), P(), P())
    return jax.shard_map(local, mesh=finer, in_specs=in_specs, out_specs=out_specs, check_vma=False)
```

profile of v0, /device:TPU:1, one launch (start us, length us, event | category | flops | bytes accessed | tf_op | source)
XLA Modules:
  0.0 286.3 jit_solution(7088400091891341082)
XLA Ops:
  9.6 5.9 %convolution_bitcast_fusion = f32[1024,1024]{0,1:T(8,128)} fusion(bf16[1024,1024]{1,0:T(8,128)(2,1)S(1)} %copy-done, bf16[1024,512]{1,0:T(8,128)(2,1)} %param.13, bf16[1024,512]{1,0:T(8,128)(2,1)} %param.14), kind=kOutput, calls=%fused_computation.1 | convolution fusion | flops 2151677952 | bytes 8388608 | tf_op jit(solution)/shard_map/dot_general | solution.py:74
  15.7 59.1 %reduce-scatter.5.cloned.1.call-done = f32[128,1024]{0,1:T(8,128)} async-done(((f32[1024,1024]{0,1:T(8,128)}), f32[128,1024]{0,1:T(8,128)}) %reduce-scatter.5.cloned.1.call-update) | async-done | bytes 524304 | tf_op jit(solution)/shard_map/reduce_scatter | solution.py:14
  74.8 2.0 copy.44
  77.0 21.9 %reduce-scatter.7.cloned.1.call-done = f32[32,1024]{1,0:T(8,128)} async-done(((f32[128,1024]{1,0:T(8,128)}), f32[32,1024]{1,0:T(8,128)}) %reduce-scatter.7.cloned.1.call-update) | async-done | bytes 131088 | tf_op jit(solution)/shard_map/reduce_scatter | solution.py:14
  102.6 2.0 convolution_subtract_fusion
  106.7 2.8 convolution_bitcast_fusion.1
  109.5 2.5 copy.38
  112.0 2.8 concatenate.17
  116.2 2.8 convolution_bitcast_fusion.2
  122.2 2.1 maximum_bitcast_fusion
  125.5 27.3 %all_to_all.28 = f32[4,64,2048]{2,1,0:T(8,128)} all-to-all(f32[4,64,2048]{2,1,0:T(8,128)S(1)} %copy.39), channel_id=1, replica_groups=mesh['row_0'=4,'row_1'=2,'col_0'=8,'col_1'=4] {'col_1'}, dimensions={0} | all-to-all | bytes 4194304 | tf_op jit(solution)/shard_map/all_to_all | solution.py:26
  152.7 1.8 reduce_sum.18
  155.6 13.3 %all-to-all-start.1 = ((f32[64,1,2048]{2,1,0:T(1,128)}), f32[64,1,2048]{2,1,0:T(1,128)S(1)}, u32[]{:S(2)}, u32[]{:S(2)}) async-start(f32[64,1,2048]{2,1,0:T(1,128)} %all_to_all.19), calls=%async_computation.2 | async-start | bytes 1048576 | tf_op jit(solution)/shard_map/all_to_all | solution.py:33
  169.2 5.9 %negate_bitcast_fusion = f32[1024,1024]{0,1:T(8,128)} fusion(bf16[1024,1024]{1,0:T(8,128)(2,1)S(1)} %copy-done, bf16[1024,512]{1,0:T(8,128)(2,1)} %param.11, bf16[1024,512]{1,0:T(8,128)(2,1)} %param.12), kind=kOutput, calls=%fused_computation | convolution fusion | flops 2152726528 | bytes 8388608 | tf_op jit(solution)/shard_map/rc,rb->cb/dot_general | solution.py:78
  175.1 10.9 %all-to-all-done.1 = f32[64,1,2048]{2,1,0:T(1,128)S(1)} async-done(((f32[64,1,2048]{2,1,0:T(1,128)}), f32[64,1,2048]{2,1,0:T(1,128)S(1)}, u32[]{:S(2)}, u32[]{:S(2)}) %all-to-all-start.1) | async-done | bytes 524320 | tf_op jit(solution)/shard_map/all_to_all | solution.py:33
  186.6 23.5 %all_to_all.29 = f32[64,1,2048]{2,1,0:T(1,128)S(1)} all-to-all(f32[64,1,2048]{2,1,0:T(1,128)S(1)} %broadcast_in_dim.11), channel_id=1, replica_groups=mesh['row_0'=4,'row_1'=2,'col_0'=8,'col_1'=4] {'row_0','row_1','col_0'}, dimensions={0} | all-to-all | bytes 1048576 | tf_op jit(solution)/shard_map/all_to_all | solution.py:43
  211.8 4.5 %all-to-all-start.3 = ((f32[4,64,2048]{2,1,0:T(8,128)}), f32[4,64,2048]{2,1,0:T(8,128)}, u32[]{:S(2)}, u32[]{:S(2)}) async-start(f32[4,64,2048]{2,1,0:T(8,128)} %broadcast_in_dim.12), calls=%async_computation.4 | async-start | bytes 4194304 | tf_op jit(solution)/shard_map/all_to_all | solution.py:43
  216.3 39.1 %all-reduce.2.cloned.1.call-done = f32[1024,1024]{0,1:T(8,128)} async-done(((f32[1024,1024]{0,1:T(8,128)}), f32[1024,1024]{0,1:T(8,128)}) %all-reduce.2.cloned.1.call-update) | async-done | bytes 4194320 | tf_op jit(solution)/shard_map/psum | solution.py:104
  255.4 4.8 %fusion.15 = (f32[1024,512]{0,1:T(8,128)}, f32[1024,512]{0,1:T(8,128)}) fusion(f32[1024,1024]{0,1:T(8,128)} %all-reduce.2.cloned.1.call-done), kind=kLoop, calls=%fused_computation.27 | loop fusion | bytes 8388608 | tf_op jit(solution)/shard_map/slice | solution.py:106
  260.2 2.9 %copy.42 = f32[1024,512]{1,0:T(8,128)} copy(f32[1024,512]{0,1:T(8,128)} %get-tuple-element.31) | data formatting | bytes 4194304
  263.1 3.0 %copy.43 = f32[1024,512]{1,0:T(8,128)} copy(f32[1024,512]{0,1:T(8,128)} %get-tuple-element.30) | data formatting | bytes 4194304
  267.4 2.7 fusion.16
  272.3 1.9 copy.40
  275.7 3.1 %select_negate_fusion = (f32[512,512]{1,0:T(8,128)}, f32[512,512]{1,0:T(8,128)}) fusion(f32[512,512]{1,0:T(8,128)} %reshape.35, f32[512,512]{1,0:T(8,128)} %reshape.34), kind=kLoop, calls=%fused_computation.12 | loop fusion | flops 1310720 | bytes 4194304 | tf_op jit(solution)/shard_map/neg | solution.py:119
  (41 shorter events, 22.2 us)
Async XLA Ops:
  8.0 1.6 copy-start
  8.0 66.8 %reduce-scatter.5.cloned.1.call-start = ((), (), s32[]{:S(2)}) async-start(), calls=%async_computation.6 | async-start | bytes 4718592 | tf_op jit(solution)/shard_map/reduce_scatter | solution.py:14
  15.5 61.4 %copy-start.7 = (bf16[32,512]{1,0:T(8,128)(2,1)S(1)}, bf16[32,512]{1,0:T(8,128)(2,1)}, u32[]{:S(2)}) copy-start(bf16[32,512]{1,0:T(8,128)(2,1)} %param.19) | copy-start | bytes 98308
  15.5 85.8 %copy-start.1 = (f32[512,512]{1,0:T(8,128)S(1)}, f32[512,512]{1,0:T(8,128)}, u32[]{:S(2)}) copy-start(f32[512,512]{1,0:T(8,128)} %param.16) | copy-start | bytes 3145732
  15.5 83.3 %reduce-scatter.7.cloned.1.call-start = ((), (), s32[]{:S(2)}) async-start(), calls=%async_computation.8 | async-start | bytes 655360 | tf_op jit(solution)/shard_map/reduce_scatter | solution.py:14
  101.3 5.3 %copy-start.2 = (f32[512,512]{1,0:T(8,128)S(1)}, f32[512,512]{1,0:T(8,128)}, u32[]{:S(2)}) copy-start(f32[512,512]{1,0:T(8,128)} %param.15) | copy-start | bytes 3145732
  102.0 0.6 copy-start.6
  104.6 0.6 copy-start.4
  155.6 30.4 %all-to-all-start.1 = ((f32[64,1,2048]{2,1,0:T(1,128)}), f32[64,1,2048]{2,1,0:T(1,128)S(1)}, u32[]{:S(2)}, u32[]{:S(2)}) async-start(f32[64,1,2048]{2,1,0:T(1,128)} %all_to_all.19), calls=%async_computation.2 | async-start | bytes 1048576 | tf_op jit(solution)/shard_map/all_to_all | solution.py:33
  168.9 86.5 %all-reduce.2.cloned.1.call-start = ((), (), s32[]{:S(2)}) async-start(), calls=%async_computation.7 | async-start | bytes 8388608 | tf_op jit(solution)/shard_map/psum | solution.py:104
  211.8 55.6 %all-to-all-start.3 = ((f32[4,64,2048]{2,1,0:T(8,128)}), f32[4,64,2048]{2,1,0:T(8,128)}, u32[]{:S(2)}, u32[]{:S(2)}) async-start(f32[4,64,2048]{2,1,0:T(8,128)} %broadcast_in_dim.12), calls=%async_computation.4 | async-start | bytes 4194304 | tf_op jit(solution)/shard_map/all_to_all | solution.py:43
  263.1 3.0 %copy-start.3 = (f32[512,512]{1,0:T(8,128)S(1)}, f32[512,512]{1,0:T(8,128)}, u32[]{:S(2)}) copy-start(f32[512,512]{1,0:T(8,128)} %param.15) | copy-start | bytes 3145732
  263.1 3.0 %copy-start.5 = (f32[32,512]{1,0:T(8,128)S(1)}, f32[32,512]{1,0:T(8,128)}, u32[]{:S(2)}) copy-start(f32[32,512]{1,0:T(8,128)} %copy-done.4) | copy-start | bytes 196612
Sparse Core Ops, SparseCore 0:
  15.6 59.1 reduce-scatter.4
  77.9 20.9 reduce-scatter.6
Sparse Core Ops, SparseCore 1:
  175.2 80.2 all-reduce.1
where the time goes:
time: 288 us; the launch traced here: 286 us
  waiting for transfers between devices  131 us (45%)
  blocking collectives  50.7 us (18%)
  local copies, waits for them, and re-layouts  39.3 us (14%)
  matrix products  24.1 us (8%)
  starting transfers between devices  18.3 us (6%)
  between operations  15.7 us (5%)
  other arithmetic  7.28 us (3%)
    reduce_scatter x2, waiting for transfers between devices, summed_rows(): total = lax.psum_scatter(total, axis, scatter_dimension=0, tiled=True)  80.9 us
    psum x1, waiting for transfers between devices, local(): column_sum = lax.psum(column_term(adj_trailing, both_rows), ROW)  39.1 us
    all_to_all x1, blocking collectives, sum_at_owner(): lax.all_to_all(in_blocks(shard, dim, length), axis, 0, 0, tiled=True)  27.3 us
    all_to_all x1, blocking collectives, sent_to_all(): return lax.all_to_all(copies, axis, split_axis=0, concat_axis=0, tiled=True)  23.5 us
    all_to_all x1, starting transfers between devices, sum_by_axis(): return jnp.sum(lax.all_to_all(own, far, 0, 0, tiled=True), axis=0)  13.3 us
    unnamed x22, local copies, waits for them, and re-layouts  11.9 us
    all_to_all x1, waiting for transfers between devices, sum_by_axis(): return jnp.sum(lax.all_to_all(own, far, 0, 0, tiled=True), axis=0)  10.9 us
    dot_general x1, matrix products, column_term(): jnp.einsum('rc,rb->cb', adj_trailing, rows, preferred_element_type=jnp.fl...  5.9 us
  transfers between devices with their start and end apart: 5, of which 4 were waited for; matrix products, arithmetic and copies ran while one was open for 7% of the time, Pallas kernels for 0%

commit v1 on v0

v1 whole, which is shorter than its diff:
```python
import jax
import jax.numpy as jnp
from jax import lax
from jax.experimental import pallas as pl
from jax.experimental.pallas import tpu as pltpu
from jax.sharding import Mesh
from jax.sharding import PartitionSpec as P

AXES = ("x", "core", "z", "y")
SIZES = (4, 2, 8, 4)
ROW = ("x", "core")
COL = ("z", "y")
F32 = jnp.float32
BF16 = jnp.bfloat16
VMEM_LIMIT = 46 << 20
HIGHEST = lax.Precision.HIGHEST
TILES = [(i, j) for i in range(4) for j in range(i + 1)]

Z_FIRST = 1

ORDER = (
    *("a1", "b0", "x3", "x1", "x2", "x0", "g", "a1", "m", "d1", "a0", "d0", "a1", "x1", "d1", "x0",),
    *("d0", "a0", "x3", "x1", "b1", "b0", "d1", "a0", "d0", "d1", "x0", "a0", "x1", "b1", "d1", "d0",),
    *("a1", "x2", "x3", "x0", "b0", "d0", "a1", "b0", "d1", "x1", "x2", "a0", "b1", "a1", "x3", "x1",),
    *("b0", "b1", "d0", "x0", "b0", "b1", "d1", "x2", "a1", "a0", "x3", "d1", "b1", "x2", "b0", "x0",),
    *("d0", "x3", "a0", "b1", "r", "x2", "d0",),
)


def dot(a, b):
    return jnp.dot(a, b, preferred_element_type=F32)


def dot_t(a, b):
    return lax.dot_general(a, b, (((0,), (0,)), ((), ())), preferred_element_type=F32)


def dot_f32(a, b):
    return jnp.dot(a, b, precision=HIGHEST, preferred_element_type=F32)


def split(v):
    high = v.astype(BF16)
    return high, (v - high.astype(F32)).astype(BF16)


def dot_t2(a, b):
    high, low = split(b)
    return dot_t(a, high) + dot_t(a, low)


def dot_t3(a, b):
    ah, al = split(a)
    bh, bl = split(b)
    return dot_t(ah, bh) + (dot_t(ah, bl) + dot_t(al, bh))


def plus(axis, step):
    size = SIZES[AXES.index(axis)]
    return lax.rem(lax.axis_index(axis) + (size + step), size)


def kernel(
    a_in, r0_in, r1_in, k0_in, k1_in, inv0_in, inv1_in, cross_in, p0_in, p1_in,
    col, d_all, rows,
    a_v, r_v, k_v, inv1, inv0, cross, p1_v, p0_v,
    c_send, c_recv, c_sum, x1_recv, x2_recv,
    t_z, zz_recv, t_zy, zy1_recv, zy2_recv,
    t_y, yy1_recv, yy2_recv, t_yz, yz_recv, trail,
    g_v, d_part, d_core, d_sum, d_y, dy_recv, dz_recv, d_x,
    local_sem, send_sem, recv_sem,
):
    x, core, z, y = (lax.axis_index(axis) for axis in AXES)
    xp, xm, xf = plus("x", 1), plus("x", -1), plus("x", 2)
    yp, ym, yf = plus("y", 1), plus("y", -1), plus("y", 2)
    other = 1 - core
    sent, locals_ = [], []

    def send(src, dst, **peer):
        at = len(sent)
        copy = pltpu.make_async_remote_copy(
            src_ref=src, dst_ref=dst, send_sem=send_sem.at[at], recv_sem=recv_sem.at[at],
            device_id=peer, device_id_type=pl.DeviceIdType.MESH,
        )
        copy.start()
        sent.append(copy)
        return copy

    def copy_in(src, dst):
        copy = pltpu.make_async_copy(src, dst, local_sem.at[len(locals_)])
        copy.start()
        locals_.append(copy)
        return copy

    in_r = [copy_in(r1_in, r_v.at[:, 0:512]), copy_in(r0_in, r_v.at[:, 512:1024])]
    in_a = copy_in(a_in, a_v)
    in_k = [copy_in(k1_in, k_v.at[:, 0:512]), copy_in(k0_in, k_v.at[:, 512:1024])]
    in_p = [copy_in(p1_in, p1_v), copy_in(p0_in, p0_v)]
    in_m = [copy_in(inv1_in, inv1), copy_in(cross_in, cross), copy_in(inv0_in, inv0)]

    barrier = pltpu.get_barrier_semaphore()
    peers = [{"core": other}]
    peers += [{"x": plus("x", s)} for s in (1, 2, 3)]
    peers += [{"y": plus("y", s)} for s in (1, 2, 3)]
    peers += [{"z": plus("z", s)} for s in range(1, 8)]
    for peer in peers:
        pl.semaphore_signal(barrier, inc=1, device_id=peer, device_id_type=pl.DeviceIdType.MESH)

    def half(index):
        return pl.ds(pl.multiple_of(index * 512, 512), 512)

    for copy in (*in_r, in_a):
        copy.wait()
    to_core = []
    for j in range(4):
        c_send[j] = -dot_t(a_v[:, half(other)], r_v[:, 256 * j : 256 * j + 256])
        if j == 0:
            pl.semaphore_wait(barrier, len(peers))
        to_core.append(send(c_send.at[j], c_recv.at[j], core=other))
    for j in range(4):
        c_sum[j] = -dot_t(a_v[:, half(core)], r_v[:, 256 * j : 256 * j + 256])

    def rows_at(index, size, extra=0, count=None):
        start = pl.multiple_of(index * size + extra, 8)
        return pl.ds(start, size if count is None else count)

    def x_stream(j):
        to_core[j].wait_recv()
        c_sum[j] = c_sum[j] + c_recv[j]
        p = send(c_sum.at[j, rows_at(xf, 128, 0, 64)], x1_recv.at[j, 0], x=xp)
        m = send(c_sum.at[j, rows_at(xf, 128, 64, 64)], x1_recv.at[j, 1], x=xm)
        yield
        p.wait_recv()
        at = rows_at(xp, 128, 0, 64)
        c_sum[j, at] = c_sum[j, at] + x1_recv[j, 0]
        p = send(c_sum.at[j, rows_at(xp, 128)], x2_recv.at[j, 0], x=xp)
        m.wait_recv()
        at = rows_at(xm, 128, 64, 64)
        c_sum[j, at] = c_sum[j, at] + x1_recv[j, 1]
        m = send(c_sum.at[j, rows_at(xm, 128)], x2_recv.at[j, 1], x=xm)
        yield
        p.wait_recv()
        m.wait_recv()
        base = core * 512
        own = pl.ds(pl.multiple_of(base + x * 128, 128), 128)
        col[j, own] = c_sum[j, rows_at(x, 128)] + x2_recv[j, 0] + x2_recv[j, 1]
        p = send(col.at[j, own], col.at[j, own], x=xp)
        m = send(col.at[j, own], col.at[j, own], x=xm)
        yield
        p.wait_recv()
        at = pl.ds(pl.multiple_of(base + xm * 128, 64), 64)
        p = send(col.at[j, at], col.at[j, at], x=xp)
        m.wait_recv()
        at = pl.ds(pl.multiple_of(base + xp * 128 + 64, 64), 64)
        m = send(col.at[j, at], col.at[j, at], x=xm)
        yield
        p.wait_recv()
        m.wait_recv()
        c = send(col.at[j, half(core)], col.at[j, half(core)], core=other)
        yield
        c.wait_recv()
        yield

    def z_ring(q, recv, size):
        h = size // 2
        far = plus("z", 4)
        p = send(q.at[far, 0:h], recv.at[0, 0, 0:h], z=plus("z", 1))
        m = send(q.at[far, h:size], recv.at[1, 0, 0:h], z=plus("z", -1))
        yield
        for s in (1, 2, 3):
            to_p, to_m = plus("z", 4 - s), plus("z", s - 4)
            p.wait_recv()
            if s == 1:
                q[to_p, 0:h] = q[to_p, 0:h] + recv[0, 0, 0:h]
            else:
                q[to_p] = q[to_p] + recv[0, s - 1]
            p = send(q.at[to_p], recv.at[0, s], z=plus("z", 1))
            m.wait_recv()
            if s == 1:
                q[to_m, h:size] = q[to_m, h:size] + recv[1, 0, 0:h]
            else:
                q[to_m] = q[to_m] + recv[1, s - 1]
            m = send(q.at[to_m], recv.at[1, s], z=plus("z", -1))
            yield
        p.wait_recv()
        m.wait_recv()

    z_panel, y_panel = (0, 1) if Z_FIRST == 1 else (1, 0)

    def a_stream(i):
        lanes = slice(256 * i, 256 * i + 256)
        first = 512 * z_panel + 256 * i
        t, ty = t_z.at[i], t_zy.at[i]
        t[...] = dot(a_v[...], k_v[:, first : first + 256]).reshape(8, 128, 256)
        yield from z_ring(t, zz_recv.at[i], 128)
        ty[...] = (t[z] + zz_recv[i, 0, 3] + zz_recv[i, 1, 3]).reshape(4, 32, 256)
        p = send(ty.at[yf, 0:16], zy1_recv.at[i, 0], y=yp)
        m = send(ty.at[yf, 16:32], zy1_recv.at[i, 1], y=ym)
        yield
        p.wait_recv()
        ty[yp, 0:16] = ty[yp, 0:16] + zy1_recv[i, 0]
        p = send(ty.at[yp], zy2_recv.at[i, 0], y=yp)
        m.wait_recv()
        ty[ym, 16:32] = ty[ym, 16:32] + zy1_recv[i, 1]
        m = send(ty.at[ym], zy2_recv.at[i, 1], y=ym)
        yield
        p.wait_recv()
        m.wait_recv()
        trail[z_panel, :, lanes] = ty[y] + zy2_recv[i, 0] + zy2_recv[i, 1]
        yield

    def b_stream(i):
        lanes = slice(256 * i, 256 * i + 256)
        first = 512 * y_panel + 256 * i
        t, tz = t_y.at[i], t_yz.at[i]
        t[...] = dot(a_v[...], k_v[:, first : first + 256]).reshape(8, 4, 32, 256)
        p = send(t.at[0:4, yf], yy1_recv.at[i, 0], y=yp)
        m = send(t.at[4:8, yf], yy1_recv.at[i, 1], y=ym)
        yield
        p.wait_recv()
        t[0:4, yp] = t[0:4, yp] + yy1_recv[i, 0]
        p = send(t.at[:, yp], yy2_recv.at[i, 0], y=yp)
        m.wait_recv()
        t[4:8, ym] = t[4:8, ym] + yy1_recv[i, 1]
        m = send(t.at[:, ym], yy2_recv.at[i, 1], y=ym)
        yield
        p.wait_recv()
        m.wait_recv()
        tz[...] = t[:, y] + yy2_recv[i, 0] + yy2_recv[i, 1]
        yield from z_ring(tz, yz_recv.at[i], 32)
        trail[y_panel, :, lanes] = tz[z] + yz_recv[i, 0, 3] + yz_recv[i, 1, 3]
        yield

    def gram():
        at = pl.ds(pl.multiple_of((z * 4 + y) * 32, 32), 32)
        k1, k0 = k_v[half(core), 0:512], k_v[half(core), 512:1024]
        r1, r0 = r_v[at, 0:512], r_v[at, 512:1024]
        p1, p0 = p1_v[...], p0_v[...]
        g_v[0, :, 0:256] = dot_t2(k1, c_sum[0]) + dot_t(p1, r1[:, 0:256])
        g_v[0, 256:512, 256:512] = dot_t2(k1[:, 256:512], c_sum[1]) + dot_t(p1[:, 256:512], r1[:, 256:512])
        for j in (0, 1):
            lanes = slice(256 * j, 256 * j + 256)
            g_v[1, :, lanes] = dot_t2(k1, c_sum[2 + j]) + dot_t(p1, r0[:, lanes])
        g_v[2, :, 0:256] = dot_t2(k0, c_sum[2]) + dot_t(p0, r0[:, 0:256])
        g_v[2, 256:512, 256:512] = dot_t2(k0[:, 256:512], c_sum[3]) + dot_t(p0[:, 256:512], r0[:, 256:512])

    def lower_t(inv, g, whole):
        upper = dot_t3(inv[:, 0:256], g[:, 0:512] if whole else g[:, 0:256])
        lower = dot_t3(inv[256:512, 256:512], g[256:512, 0:512])
        return upper, lower

    def put_tiles(at, upper, lower):
        for index, (i, j) in enumerate(TILES):
            v = upper if i < 2 else lower
            v = v[128 * (i % 2) : 128 * (i % 2) + 128, 128 * j : 128 * j + 128]
            if i == j:
                row = lax.broadcasted_iota(jnp.int32, (128, 128), 0)
                lane = lax.broadcasted_iota(jnp.int32, (128, 128), 1)
                v = jnp.where(row >= lane, v, 0.0)
            d_part[at, 128 * index : 128 * index + 128] = -v

    def local_diag():
        put_tiles(0, *lower_t(inv1[...], g_v[0], False))
        w_upper, w_lower = lower_t(inv1[...], g_v[1], True)
        g_v[1, 0:256] = w_upper
        g_v[1, 256:512] = w_lower
        g_v[2, :, 0:256] = g_v[2, :, 0:256] - dot_t3(cross[...], g_v[1, :, 0:256])
        g_v[2, 256:512, 256:512] = g_v[2, 256:512, 256:512] - dot_t3(cross[:, 256:512], g_v[1, :, 256:512])
        put_tiles(1, *lower_t(inv0[...], g_v[2], False))

    def d_stream(i):
        size, base = (768, 512)[i], (0, 768)[i]
        ny, nz = size // 4, size // 32
        whole, by, bz = pl.ds(base, size), pl.ds(base // 4, ny), pl.ds(base // 32, nz)

        def of_y(index, start):
            return pl.ds(pl.multiple_of(start + index * ny, 8), ny)

        def of_z(index, start):
            return pl.ds(pl.multiple_of(start + index * nz, 8), nz)

        c = send(d_part.at[other, whole], d_core.at[whole], core=other)
        yield
        c.wait_recv()
        d_sum[whole] = d_part[core, whole] + d_core[whole]
        cs = [send(d_sum.at[of_y(plus("y", s), base)], dy_recv.at[s - 1, by], y=plus("y", s)) for s in (1, 2, 3)]
        yield
        for c in cs:
            c.wait_recv()
        d_y[by] = d_sum[of_y(y, base)] + dy_recv[0, by] + dy_recv[1, by] + dy_recv[2, by]
        cs = [send(d_y.at[of_z(plus("z", s), base // 4)], dz_recv.at[s - 1, bz], z=plus("z", s)) for s in range(1, 8)]
        yield
        for c in cs:
            c.wait_recv()
        total = d_y[of_z(z, base // 4)]
        for s in range(7):
            total = total + dz_recv[s, bz]
        d_x[x, bz] = total
        cs = [send(d_x.at[x, bz], d_x.at[x, bz], x=plus("x", s)) for s in (1, 2, 3)]
        yield
        for c in cs:
            c.wait_recv()
        own = pl.ds(pl.multiple_of(base + y * ny + z * nz, 8), nz)
        d_all[core, own] = (d_x[0, bz] + d_x[1, bz]) + (d_x[2, bz] + d_x[3, bz])
        cs = [send(d_all.at[core, own], d_all.at[core, own], z=plus("z", s)) for s in range(1, 8)]
        yield
        for c in cs:
            c.wait_recv()
        own = of_y(y, base)
        cs = [send(d_all.at[core, own], d_all.at[core, own], y=plus("y", s)) for s in (1, 2, 3)]
        yield
        for c in cs:
            c.wait_recv()
        c = send(d_all.at[core, whole], d_all.at[core, whole], core=other)
        yield
        c.wait_recv()
        yield

    def row_adjoints():
        bar1 = p1_v[...].astype(F32) - trail[0]
        row1 = dot_f32(bar1, inv1[...])
        rows[0] = row1
        bar0 = p0_v[...].astype(F32) - trail[1] - dot_f32(row1, cross[...])
        rows[1] = dot_f32(bar0, inv0[...])

    streams = {"x%d" % j: x_stream(j) for j in range(4)}
    for i in range(2):
        streams.update({"a%d" % i: a_stream(i), "b%d" % i: b_stream(i), "d%d" % i: d_stream(i)})
    loaded = len(in_r) + 1
    for name in ORDER:
        if name[0] in "ab" and loaded < len(locals_):
            for copy in locals_[loaded:]:
                copy.wait()
            loaded = len(locals_)
        if name == "g":
            gram()
        elif name == "m":
            local_diag()
        elif name == "r":
            row_adjoints()
        else:
            next(streams[name])
    for copy in sent:
        copy.wait_send()


def place(col, d_all, rows, row1_out, row0_out, col1_out, col0_out, diag1_out, diag0_out, diag, sem):
    copies = []

    def put(src, dst):
        copy = pltpu.make_async_copy(src, dst, sem.at[len(copies)])
        copy.start()
        copies.append(copy)

    for j in range(4):
        out = (col1_out, col0_out)[j // 2]
        put(col.at[j], out.at[:, 256 * (j % 2) : 256 * (j % 2) + 256])
    put(rows.at[0], row1_out)
    put(rows.at[1], row0_out)
    for panel, out in enumerate((diag1_out, diag0_out)):
        for i in range(3):
            diag[panel, 128 * i : 128 * i + 128, 128 * i + 128 : 512] = jnp.zeros((128, 384 - 128 * i), F32)
        for index, (i, j) in enumerate(TILES):
            tile = d_all[panel, 128 * index : 128 * index + 128]
            diag[panel, 128 * i : 128 * i + 128, 128 * j : 128 * j + 128] = tile
        put(diag.at[panel], out)
    for copy in copies:
        copy.wait()


def local(adj_trailing, panel_rows0, panel_rows1, panel_cols0, panel_cols1, inv_diag0, inv_diag1, cross_block, panel_adj0, panel_adj1):
    anywhere = pl.BlockSpec(memory_space=pltpu.HBM)
    vmem = pl.BlockSpec(memory_space=pltpu.VMEM)
    out = lambda *dims: jax.ShapeDtypeStruct(dims, F32)
    f = lambda *dims: pltpu.VMEM(dims, F32)
    b = lambda *dims: pltpu.VMEM(dims, BF16)
    results = pl.pallas_call(
        kernel,
        out_shape=(f(4, 1024, 256), f(2, 1280, 128), f(2, 32, 512)),
        in_specs=[anywhere] * 10,
        out_specs=(vmem,) * 3,
        scratch_shapes=[
            b(1024, 1024), b(1024, 1024), b(1024, 1024), f(512, 512), f(512, 512), f(512, 512), b(32, 512), b(32, 512),
            f(4, 512, 256), f(4, 512, 256), f(4, 512, 256), f(4, 2, 64, 256), f(4, 2, 128, 256),
            f(2, 8, 128, 256), f(2, 2, 4, 128, 256), f(2, 4, 32, 256), f(2, 2, 16, 256), f(2, 2, 32, 256),
            f(2, 8, 4, 32, 256), f(2, 2, 4, 32, 256), f(2, 2, 8, 32, 256), f(2, 8, 32, 256), f(2, 2, 4, 32, 256), f(2, 32, 512),
            f(3, 512, 512), f(2, 1280, 128), f(1280, 128), f(1280, 128), f(320, 128), f(3, 320, 128),
            f(7, 40, 128), f(4, 40, 128),
            pltpu.SemaphoreType.DMA((16,)), pltpu.SemaphoreType.DMA((152,)), pltpu.SemaphoreType.DMA((152,)),
        ],
        compiler_params=pltpu.CompilerParams(collective_id=0, has_side_effects=True, vmem_limit_bytes=VMEM_LIMIT),
        name="panels",
    )(
        adj_trailing, panel_rows0, panel_rows1, panel_cols0, panel_cols1,
        inv_diag0, inv_diag1, cross_block, panel_adj0, panel_adj1,
    )
    return pl.pallas_call(
        place,
        out_shape=(out(32, 512), out(32, 512), out(1024, 512), out(1024, 512), out(512, 512), out(512, 512)),
        in_specs=[vmem] * 3,
        out_specs=(anywhere,) * 6,
        scratch_shapes=[f(2, 512, 512), pltpu.SemaphoreType.DMA((8,))],
        compiler_params=pltpu.CompilerParams(vmem_limit_bytes=4 << 20),
        name="place",
    )(*results)


def solution(mesh):
    finer = Mesh(mesh.devices.reshape(SIZES), AXES)
    every = (*ROW, *COL)
    in_specs = (
        P(ROW, COL), P(ROW, None), P(ROW, None), P(COL, None), P(COL, None),
        P(), P(), P(), P(every, None), P(every, None),
    )
    out_specs = (P(every, None), P(every, None), P(COL, None), P(COL, None), P(), P())
    return jax.shard_map(local, mesh=finer, in_specs=in_specs, out_specs=out_specs, check_vma=False)
```

time: 288 us -> 72.7 us (0.25)
  waiting for transfers between devices: 131 us -> 0 us
  Pallas kernels: 0 us -> 67.8 us
  blocking collectives: 50.7 us -> 0 us
  local copies, waits for them, and re-layouts: 39.3 us -> 3.96 us
  matrix products: 24.1 us -> 0 us
  starting transfers between devices: 18.3 us -> 0 us
  between operations: 15.7 us -> 0.66 us
  other arithmetic: 7.28 us -> 0 us
    reduce_scatter x2 -> x0, waiting for transfers between devices: 80.9 us -> none  [summed_rows(): total = lax.psum_scatter(total, axis, scatter_dimension=0, tiled=True)]
    pallas_call x0 -> x2, Pallas kernels: none -> 67.8 us  [the longest x1 65 us: local(): pl.pallas_call(kernel, out_shape=(f(4, 1024, 256), f(2, 1280, 128), f(2,...]
    all_to_all x2 -> x0, blocking collectives: 50.7 us -> none  [the longest x1 27.3 us: sum_at_owner(): lax.all_to_all(in_blocks(shard, dim, length), axis, 0, 0, tiled=True)]
    psum x1 -> x0, waiting for transfers between devices: 39.1 us -> none  [local(): column_sum = lax.psum(column_term(adj_trailing, both_rows), ROW)]
    dot_general x9 -> x0, matrix products: 24.1 us -> none  [the longest x1 5.9 us: column_term(): jnp.einsum('rc,rb->cb', adj_trailing, rows, preferred_element_type=jnp.fl...]
    all_to_all x2 -> x0, starting transfers between devices: 17.8 us -> none  [the longest x1 13.3 us: sum_by_axis(): return jnp.sum(lax.all_to_all(own, far, 0, 0, tiled=True), axis=0)]
    slice x5 -> x0, local copies, waits for them, and re-layouts: 11.6 us -> none  [the longest x3 5.27 us: packed_total(): outs.append(total[at:at + a.size].reshape(a.shape))]
    all_to_all x2 -> x0, waiting for transfers between devices: 10.9 us -> none  [the longest x1 10.9 us: sum_by_axis(): return jnp.sum(lax.all_to_all(own, far, 0, 0, tiled=True), axis=0)]
  transfers between devices with their start and end apart: 5 -> 0, of which waited for: 4 -> 0; matrix products, arithmetic and copies ran while one was open for 7% -> 0% of each run, Pallas kernels for 0% -> 0%
where the time goes in v1:
time: 72.7 us; the launch traced here: 72.4 us
  Pallas kernels  67.8 us (93%)
  local copies, waits for them, and re-layouts  3.96 us (5%)
    pallas_call x1, Pallas kernels, local(): pl.pallas_call(kernel, out_shape=(f(4, 1024, 256), f(2, 1280, 128), f(2,...  65 us
    unnamed x8, local copies, waits for them, and re-layouts  3.96 us
    pallas_call x1, Pallas kernels, local(): pl.pallas_call(place, out_shape=(out(32, 512), out(32, 512), out(1024, 51...  2.78 us

profile of v1, /device:TPU:1, one launch (start us, length us, event | category | flops | bytes accessed | tf_op | source)
XLA Modules:
  0.0 72.4 jit_solution(15560463712037148557)
XLA Ops:
  0.6 0.0 copy-start
  0.6 1.2 %copy-done = bf16[1024,512]{1,0:T(8,128)(2,1)S(1)} copy-done((bf16[1024,512]{1,0:T(8,128)(2,1)S(1)}, bf16[1024,512]{1,0:T(8,128)(2,1)}, u32[]{:S(2)}) %copy-start) | copy-done | bytes 1048600
  1.9 0.0 copy-start.1
  1.9 1.2 %copy-done.1 = bf16[1024,512]{1,0:T(8,128)(2,1)S(1)} copy-done((bf16[1024,512]{1,0:T(8,128)(2,1)S(1)}, bf16[1024,512]{1,0:T(8,128)(2,1)}, u32[]{:S(2)}) %copy-start.1) | copy-done | bytes 1048600
  3.1 0.0 copy-start.2
  3.1 0.8 %copy-done.2 = bf16[32,512]{1,0:T(8,128)(2,1)S(1)} copy-done((bf16[32,512]{1,0:T(8,128)(2,1)S(1)}, bf16[32,512]{1,0:T(8,128)(2,1)}, u32[]{:S(2)}) %copy-start.2) | copy-done | bytes 32792
  3.8 0.0 copy-start.3
  3.8 0.8 %copy-done.3 = bf16[32,512]{1,0:T(8,128)(2,1)S(1)} copy-done((bf16[32,512]{1,0:T(8,128)(2,1)S(1)}, bf16[32,512]{1,0:T(8,128)(2,1)}, u32[]{:S(2)}) %copy-start.3) | copy-done | bytes 32792
  4.6 65.0 %panels.1 = (f32[4,1024,256]{2,1,0:T(8,128)S(1)}, f32[2,1280,128]{2,1,0:T(8,128)S(1)}, f32[2,32,512]{2,1,0:T(8,128)S(1)}) custom-call(bf16[1024,1024]{1,0:T(8,128)(2,1)} %a_in.1, bf16[1024,512]{1,0:T(8,128)(2,1)S(1)} %copy-done, bf16[1024,512]{1,0:T(8,128)(2,1)S(1)} %copy-done.1, bf16[1024,512]{1,0:T(8,128)(2,1)} %k0_in.1, bf16[1024,512]{1,0:T(8,128)(2,1)} %k1_in.1, ...), custom_call_target="tpu_custom_call" | custom-call | tf_op jit(solution)/shard_map/panels/pallas_call | solution.py:377
  69.6 2.8 %place.1 = (f32[32,512]{1,0:T(8,128)}, f32[32,512]{1,0:T(8,128)}, f32[1024,512]{1,0:T(8,128)}, f32[1024,512]{1,0:T(8,128)}, f32[512,512]{1,0:T(8,128)}, /*index=5*/f32[512,512]{1,0:T(8,128)}) custom-call(f32[4,1024,256]{2,1,0:T(8,128)S(1)} %get-tuple-element.9.col, f32[2,1280,128]{2,1,0:T(8,128)S(1)} %get-tuple-element.10.d_all, ...), custom_call_target="tpu_custom_call" | custom-call | tf_op jit(solution)/shard_map/place/pallas_call | solution.py:397
Async XLA Ops:
  0.6 1.2 %copy-start = (bf16[1024,512]{1,0:T(8,128)(2,1)S(1)}, bf16[1024,512]{1,0:T(8,128)(2,1)}, u32[]{:S(2)}) copy-start(bf16[1024,512]{1,0:T(8,128)(2,1)} %r0_in.1) | copy-start | bytes 3145732
  1.9 1.2 %copy-start.1 = (bf16[1024,512]{1,0:T(8,128)(2,1)S(1)}, bf16[1024,512]{1,0:T(8,128)(2,1)}, u32[]{:S(2)}) copy-start(bf16[1024,512]{1,0:T(8,128)(2,1)} %r1_in.1) | copy-start | bytes 3145732
  3.1 0.8 %copy-start.2 = (bf16[32,512]{1,0:T(8,128)(2,1)S(1)}, bf16[32,512]{1,0:T(8,128)(2,1)}, u32[]{:S(2)}) copy-start(bf16[32,512]{1,0:T(8,128)(2,1)} %p0_in.1) | copy-start | bytes 98308
  3.8 0.8 %copy-start.3 = (bf16[32,512]{1,0:T(8,128)(2,1)S(1)}, bf16[32,512]{1,0:T(8,128)(2,1)}, u32[]{:S(2)}) copy-start(bf16[32,512]{1,0:T(8,128)(2,1)} %p1_in.1) | copy-start | bytes 98308

commit v2 on v1

--- a/solution.py
+++ b/solution.py
@@ -12,18 +12,20 @@
 COL = ("z", "y")
 F32 = jnp.float32
 BF16 = jnp.bfloat16
-VMEM_LIMIT = 46 << 20
+VMEM_LIMIT = 50 << 20
 HIGHEST = lax.Precision.HIGHEST
 TILES = [(i, j) for i in range(4) for j in range(i + 1)]
 
 Z_FIRST = 1
 
 ORDER = (
-    *("a1", "b0", "x3", "x1", "x2", "x0", "g", "a1", "m", "d1", "a0", "d0", "a1", "x1", "d1", "x0",),
-    *("d0", "a0", "x3", "x1", "b1", "b0", "d1", "a0", "d0", "d1", "x0", "a0", "x1", "b1", "d1", "d0",),
-    *("a1", "x2", "x3", "x0", "b0", "d0", "a1", "b0", "d1", "x1", "x2", "a0", "b1", "a1", "x3", "x1",),
-    *("b0", "b1", "d0", "x0", "b0", "b1", "d1", "x2", "a1", "a0", "x3", "d1", "b1", "x2", "b0", "x0",),
-    *("d0", "x3", "a0", "b1", "r", "x2", "d0",),
+    *("a0", "a1", "x0", "x1", "b1", "x2", "x3", "g", "x4", "x5", "b0", "x6", "x7", "h", "a0", "m",),
+    *("d1", "x1", "a1", "d0", "x0", "x4", "x2", "d2", "x6", "d1", "a0", "d0", "d2", "x3", "b1", "x1",),
+    *("a1", "d1", "x6", "x4", "x5", "b0", "d0", "d2", "a0", "x6", "x1", "a1", "d1", "x2", "x4", "x1",),
+    *("d0", "x7", "d1", "b1", "d2", "x2", "a0", "x6", "x0", "x3", "d0", "b0", "a1", "x5", "x4", "x7",),
+    *("a0", "b1", "d2", "x0", "d1", "b0", "x1", "x3", "b1", "d0", "x5", "x2", "x6", "b0", "d2", "x0",),
+    *("x7", "a1", "x3", "x5", "a0", "d1", "b1", "b0", "x7", "x0", "x5", "d0", "x3", "x4", "d1", "b1",),
+    *("d2", "x2", "x7", "a1", "b0", "r", "d0", "d2",),
 )
 
 
@@ -64,7 +66,7 @@
     a_in, r0_in, r1_in, k0_in, k1_in, inv0_in, inv1_in, cross_in, p0_in, p1_in,
     col, d_all, rows,
     a_v, r_v, k_v, inv1, inv0, cross, p1_v, p0_v,
-    c_send, c_recv, c_sum, x1_recv, x2_recv,
+    c_send, c_recv, c_sum, x1_recv, x2_send, x2_recv,
     t_z, zz_recv, t_zy, zy1_recv, zy2_recv,
     t_y, yy1_recv, yy2_recv, t_yz, yz_recv, trail,
     g_v, d_part, d_core, d_sum, d_y, dy_recv, dz_recv, d_x,
@@ -92,11 +94,9 @@
         locals_.append(copy)
         return copy
 
-    in_r = [copy_in(r1_in, r_v.at[:, 0:512]), copy_in(r0_in, r_v.at[:, 512:1024])]
+    in_r1 = copy_in(r1_in, r_v.at[:, 0:512])
     in_a = copy_in(a_in, a_v)
-    in_k = [copy_in(k1_in, k_v.at[:, 0:512]), copy_in(k0_in, k_v.at[:, 512:1024])]
-    in_p = [copy_in(p1_in, p1_v), copy_in(p0_in, p0_v)]
-    in_m = [copy_in(inv1_in, inv1), copy_in(cross_in, cross), copy_in(inv0_in, inv0)]
+    in_r0 = copy_in(r0_in, r_v.at[:, 512:1024])
 
     barrier = pltpu.get_barrier_semaphore()
     peers = [{"core": other}]
@@ -109,35 +109,48 @@
     def half(index):
         return pl.ds(pl.multiple_of(index * 512, 512), 512)
 
-    for copy in (*in_r, in_a):
-        copy.wait()
+    def column_terms(index, j):
+        return -dot_t(a_v[:, half(index)], r_v[:, 256 * j : 256 * j + 256])
+
+    in_r1.wait()
+    in_a.wait()
+    copy_in(k1_in, k_v.at[:, 0:512])
+    copy_in(k0_in, k_v.at[:, 512:1024])
+    for src, dst in ((p1_in, p1_v), (p0_in, p0_v), (inv1_in, inv1), (cross_in, cross), (inv0_in, inv0)):
+        copy_in(src, dst)
     to_core = []
     for j in range(4):
-        c_send[j] = -dot_t(a_v[:, half(other)], r_v[:, 256 * j : 256 * j + 256])
+        if j == 2:
+            in_r0.wait()
+        terms = column_terms(other, j)
+        for h in range(2):
+            c_send[2 * j + h] = terms[:, 128 * h : 128 * h + 128]
         if j == 0:
             pl.semaphore_wait(barrier, len(peers))
-        to_core.append(send(c_send.at[j], c_recv.at[j], core=other))
-    for j in range(4):
-        c_sum[j] = -dot_t(a_v[:, half(core)], r_v[:, 256 * j : 256 * j + 256])
+        to_core += [send(c_send.at[at], c_recv.at[at], core=other) for at in (2 * j, 2 * j + 1)]
 
     def rows_at(index, size, extra=0, count=None):
         start = pl.multiple_of(index * size + extra, 8)
         return pl.ds(start, size if count is None else count)
 
     def x_stream(j):
+        if j % 2 == 0:
+            terms = column_terms(core, j // 2)
+            c_sum[j] = terms[:, 0:128]
+            c_sum[j + 1] = terms[:, 128:256]
         to_core[j].wait_recv()
         c_sum[j] = c_sum[j] + c_recv[j]
         p = send(c_sum.at[j, rows_at(xf, 128, 0, 64)], x1_recv.at[j, 0], x=xp)
         m = send(c_sum.at[j, rows_at(xf, 128, 64, 64)], x1_recv.at[j, 1], x=xm)
         yield
         p.wait_recv()
-        at = rows_at(xp, 128, 0, 64)
-        c_sum[j, at] = c_sum[j, at] + x1_recv[j, 0]
-        p = send(c_sum.at[j, rows_at(xp, 128)], x2_recv.at[j, 0], x=xp)
-        m.wait_recv()
-        at = rows_at(xm, 128, 64, 64)
-        c_sum[j, at] = c_sum[j, at] + x1_recv[j, 1]
-        m = send(c_sum.at[j, rows_at(xm, 128)], x2_recv.at[j, 1], x=xm)
+        x2_send[j, 0, 0:64] = c_sum[j, rows_at(xp, 128, 0, 64)] + x1_recv[j, 0]
+        x2_send[j, 0, 64:128] = c_sum[j, rows_at(xp, 128, 64, 64)]
+        p = send(x2_send.at[j, 0], x2_recv.at[j, 0], x=xp)
+        m.wait_recv()
+        x2_send[j, 1, 0:64] = c_sum[j, rows_at(xm, 128, 0, 64)]
+        x2_send[j, 1, 64:128] = c_sum[j, rows_at(xm, 128, 64, 64)] + x1_recv[j, 1]
+        m = send(x2_send.at[j, 1], x2_recv.at[j, 1], x=xm)
         yield
         p.wait_recv()
         m.wait_recv()
@@ -231,18 +244,25 @@
         trail[y_panel, :, lanes] = tz[z] + yz_recv[i, 0, 3] + yz_recv[i, 1, 3]
         yield
 
-    def gram():
-        at = pl.ds(pl.multiple_of((z * 4 + y) * 32, 32), 32)
+    def own_rows():
+        return pl.ds(pl.multiple_of((z * 4 + y) * 32, 32), 32)
+
+    def sums(j):
+        return jnp.concatenate((c_sum[2 * j], c_sum[2 * j + 1]), axis=1)
+
+    def gram1():
+        k1, r1, p1 = k_v[half(core), 0:512], r_v[own_rows(), 0:512], p1_v[...]
+        g_v[0, :, 0:256] = dot_t2(k1, sums(0)) + dot_t(p1, r1[:, 0:256])
+        g_v[0, 256:512, 256:512] = dot_t2(k1[:, 256:512], sums(1)) + dot_t(p1[:, 256:512], r1[:, 256:512])
+
+    def gram0():
         k1, k0 = k_v[half(core), 0:512], k_v[half(core), 512:1024]
-        r1, r0 = r_v[at, 0:512], r_v[at, 512:1024]
-        p1, p0 = p1_v[...], p0_v[...]
-        g_v[0, :, 0:256] = dot_t2(k1, c_sum[0]) + dot_t(p1, r1[:, 0:256])
-        g_v[0, 256:512, 256:512] = dot_t2(k1[:, 256:512], c_sum[1]) + dot_t(p1[:, 256:512], r1[:, 256:512])
-        for j in (0, 1):
-            lanes = slice(256 * j, 256 * j + 256)
-            g_v[1, :, lanes] = dot_t2(k1, c_sum[2 + j]) + dot_t(p1, r0[:, lanes])
-        g_v[2, :, 0:256] = dot_t2(k0, c_sum[2]) + dot_t(p0, r0[:, 0:256])
-        g_v[2, 256:512, 256:512] = dot_t2(k0[:, 256:512], c_sum[3]) + dot_t(p0[:, 256:512], r0[:, 256:512])
+        r0, p1, p0 = r_v[own_rows(), 512:1024], p1_v[...], p0_v[...]
+        left, right = sums(2), sums(3)
+        g_v[1, :, 0:256] = dot_t2(k1, left) + dot_t(p1, r0[:, 0:256])
+        g_v[1, :, 256:512] = dot_t2(k1, right) + dot_t(p1, r0[:, 256:512])
+        g_v[2, :, 0:256] = dot_t2(k0, left) + dot_t(p0, r0[:, 0:256])
+        g_v[2, 256:512, 256:512] = dot_t2(k0[:, 256:512], right) + dot_t(p0[:, 256:512], r0[:, 256:512])
 
     def lower_t(inv, g, whole):
         upper = dot_t3(inv[:, 0:256], g[:, 0:512] if whole else g[:, 0:256])
@@ -269,7 +289,7 @@
         put_tiles(1, *lower_t(inv0[...], g_v[2], False))
 
     def d_stream(i):
-        size, base = (768, 512)[i], (0, 768)[i]
+        size, base = (512, 512, 256)[i], 512 * i
         ny, nz = size // 4, size // 32
         whole, by, bz = pl.ds(base, size), pl.ds(base // 4, ny), pl.ds(base // 32, nz)
 
@@ -323,17 +343,20 @@
         bar0 = p0_v[...].astype(F32) - trail[1] - dot_f32(row1, cross[...])
         rows[1] = dot_f32(bar0, inv0[...])
 
-    streams = {"x%d" % j: x_stream(j) for j in range(4)}
+    streams = {"x%d" % j: x_stream(j) for j in range(8)}
+    streams.update({"d%d" % i: d_stream(i) for i in range(3)})
     for i in range(2):
-        streams.update({"a%d" % i: a_stream(i), "b%d" % i: b_stream(i), "d%d" % i: d_stream(i)})
-    loaded = len(in_r) + 1
+        streams.update({"a%d" % i: a_stream(i), "b%d" % i: b_stream(i)})
+    loaded = 3
     for name in ORDER:
-        if name[0] in "ab" and loaded < len(locals_):
+        if name[0] in "abgh" and loaded < len(locals_):
             for copy in locals_[loaded:]:
                 copy.wait()
             loaded = len(locals_)
         if name == "g":
-            gram()
+            gram1()
+        elif name == "h":
+            gram0()
         elif name == "m":
             local_diag()
         elif name == "r":
@@ -352,9 +375,9 @@
         copy.start()
         copies.append(copy)
 
-    for j in range(4):
-        out = (col1_out, col0_out)[j // 2]
-        put(col.at[j], out.at[:, 256 * (j % 2) : 256 * (j % 2) + 256])
+    for j in range(8):
+        out = (col1_out, col0_out)[j // 4]
+        put(col.at[j], out.at[:, 128 * (j % 4) : 128 * (j % 4) + 128])
     put(rows.at[0], row1_out)
     put(rows.at[1], row0_out)
     for panel, out in enumerate((diag1_out, diag0_out)):
@@ -376,17 +399,17 @@
     b = lambda *dims: pltpu.VMEM(dims, BF16)
     results = pl.pallas_call(
         kernel,
-        out_shape=(f(4, 1024, 256), f(2, 1280, 128), f(2, 32, 512)),
+        out_shape=(f(8, 1024, 128), f(2, 1280, 128), f(2, 32, 512)),
         in_specs=[anywhere] * 10,
         out_specs=(vmem,) * 3,
         scratch_shapes=[
             b(1024, 1024), b(1024, 1024), b(1024, 1024), f(512, 512), f(512, 512), f(512, 512), b(32, 512), b(32, 512),
-            f(4, 512, 256), f(4, 512, 256), f(4, 512, 256), f(4, 2, 64, 256), f(4, 2, 128, 256),
+            f(8, 512, 128), f(8, 512, 128), f(8, 512, 128), f(8, 2, 64, 128), f(8, 2, 128, 128), f(8, 2, 128, 128),
             f(2, 8, 128, 256), f(2, 2, 4, 128, 256), f(2, 4, 32, 256), f(2, 2, 16, 256), f(2, 2, 32, 256),
             f(2, 8, 4, 32, 256), f(2, 2, 4, 32, 256), f(2, 2, 8, 32, 256), f(2, 8, 32, 256), f(2, 2, 4, 32, 256), f(2, 32, 512),
             f(3, 512, 512), f(2, 1280, 128), f(1280, 128), f(1280, 128), f(320, 128), f(3, 320, 128),
             f(7, 40, 128), f(4, 40, 128),
-            pltpu.SemaphoreType.DMA((16,)), pltpu.SemaphoreType.DMA((152,)), pltpu.SemaphoreType.DMA((152,)),
+            pltpu.SemaphoreType.DMA((16,)), pltpu.SemaphoreType.DMA((208,)), pltpu.SemaphoreType.DMA((208,)),
         ],
         compiler_params=pltpu.CompilerParams(collective_id=0, has_side_effects=True, vmem_limit_bytes=VMEM_LIMIT),
         name="panels",
@@ -399,7 +422,7 @@
         out_shape=(out(32, 512), out(32, 512), out(1024, 512), out(1024, 512), out(512, 512), out(512, 512)),
         in_specs=[vmem] * 3,
         out_specs=(anywhere,) * 6,
-        scratch_shapes=[f(2, 512, 512), pltpu.SemaphoreType.DMA((8,))],
+        scratch_shapes=[f(2, 512, 512), pltpu.SemaphoreType.DMA((12,))],
         compiler_params=pltpu.CompilerParams(vmem_limit_bytes=4 << 20),
         name="place",
     )(*results)

time: 72.7 us -> 69.4 us (0.955)
  local copies, waits for them, and re-layouts: 3.96 us -> 0 us
    unnamed x8 -> x0, local copies, waits for them, and re-layouts: 3.96 us -> none
    pallas_call x1, Pallas kernels: 65 us -> 65.7 us  [local(): pl.pallas_call(kernel, out_shape=(f(8, 1024, 128), f(2, 1280, 128), f(2,...]
where the time goes in v2:
time: 69.4 us; the launch traced here: 69.3 us
  Pallas kernels  68.5 us (99%)
  between operations  0.8 us (1%)
    pallas_call x1, Pallas kernels, local(): pl.pallas_call(kernel, out_shape=(f(8, 1024, 128), f(2, 1280, 128), f(2,...  65.7 us
    pallas_call x1, Pallas kernels, local(): pl.pallas_call(place, out_shape=(out(32, 512), out(32, 512), out(1024, 51...  2.81 us

profile of v2, /device:TPU:1, one launch (start us, length us, event | category | flops | bytes accessed | tf_op | source)
XLA Modules:
  0.0 69.3 jit_solution(1388538746695375649)
XLA Ops:
  0.6 65.7 %panels.1 = (f32[8,1024,128]{2,1,0:T(8,128)S(1)}, f32[2,1280,128]{2,1,0:T(8,128)S(1)}, f32[2,32,512]{2,1,0:T(8,128)S(1)}) custom-call(bf16[1024,1024]{1,0:T(8,128)(2,1)} %a_in.1, bf16[1024,512]{1,0:T(8,128)(2,1)} %r0_in.1, bf16[1024,512]{1,0:T(8,128)(2,1)} %r1_in.1, bf16[1024,512]{1,0:T(8,128)(2,1)} %k0_in.1, bf16[1024,512]{1,0:T(8,128)(2,1)} %k1_in.1, ...), custom_call_target="tpu_custom_call" | custom-call | tf_op jit(solution)/shard_map/panels/pallas_call | solution.py:400
  66.4 2.8 %place.1 = (f32[32,512]{1,0:T(8,128)}, f32[32,512]{1,0:T(8,128)}, f32[1024,512]{1,0:T(8,128)}, f32[1024,512]{1,0:T(8,128)}, f32[512,512]{1,0:T(8,128)}, /*index=5*/f32[512,512]{1,0:T(8,128)}) custom-call(f32[8,1024,128]{2,1,0:T(8,128)S(1)} %get-tuple-element.9.col, f32[2,1280,128]{2,1,0:T(8,128)S(1)} %get-tuple-element.10.d_all, ...), custom_call_target="tpu_custom_call" | custom-call | tf_op jit(solution)/shard_map/place/pallas_call | solution.py:420

commit v3 on v1

--- a/solution.py
+++ b/solution.py
@@ -12,7 +12,7 @@
 COL = ("z", "y")
 F32 = jnp.float32
 BF16 = jnp.bfloat16
-VMEM_LIMIT = 46 << 20
+VMEM_LIMIT = 50 << 20
 HIGHEST = lax.Precision.HIGHEST
 TILES = [(i, j) for i in range(4) for j in range(i + 1)]
 

time: 72.7 us -> 68.3 us (0.939)
  local copies, waits for them, and re-layouts: 3.96 us -> 0 us
    unnamed x8 -> x0, local copies, waits for them, and re-layouts: 3.96 us -> none
where the time goes in v3:
time: 68.3 us; the launch traced here: 68.2 us
  Pallas kernels  67.5 us (99%)
    pallas_call x1, Pallas kernels, local(): pl.pallas_call(kernel, out_shape=(f(4, 1024, 256), f(2, 1280, 128), f(2,...  64.7 us
    pallas_call x1, Pallas kernels, local(): pl.pallas_call(place, out_shape=(out(32, 512), out(32, 512), out(1024, 51...  2.78 us

profile of v3, /device:TPU:1, one launch (start us, length us, event | category | flops | bytes accessed | tf_op | source)
XLA Modules:
  0.0 68.2 jit_solution(18183396624583171594)
XLA Ops:
  0.6 64.7 %panels.1 = (f32[4,1024,256]{2,1,0:T(8,128)S(1)}, f32[2,1280,128]{2,1,0:T(8,128)S(1)}, f32[2,32,512]{2,1,0:T(8,128)S(1)}) custom-call(bf16[1024,1024]{1,0:T(8,128)(2,1)} %a_in.1, bf16[1024,512]{1,0:T(8,128)(2,1)} %r0_in.1, bf16[1024,512]{1,0:T(8,128)(2,1)} %r1_in.1, bf16[1024,512]{1,0:T(8,128)(2,1)} %k0_in.1, bf16[1024,512]{1,0:T(8,128)(2,1)} %k1_in.1, ...), custom_call_target="tpu_custom_call" | custom-call | tf_op jit(solution)/shard_map/panels/pallas_call | solution.py:377
  65.4 2.8 %place.1 = (f32[32,512]{1,0:T(8,128)}, f32[32,512]{1,0:T(8,128)}, f32[1024,512]{1,0:T(8,128)}, f32[1024,512]{1,0:T(8,128)}, f32[512,512]{1,0:T(8,128)}, /*index=5*/f32[512,512]{1,0:T(8,128)}) custom-call(f32[4,1024,256]{2,1,0:T(8,128)S(1)} %get-tuple-element.9.col, f32[2,1280,128]{2,1,0:T(8,128)S(1)} %get-tuple-element.10.d_all, ...), custom_call_target="tpu_custom_call" | custom-call | tf_op jit(solution)/shard_map/place/pallas_call | solution.py:397

commit v4 on v3

--- a/solution.py
+++ b/solution.py
@@ -19,11 +19,11 @@
 Z_FIRST = 1
 
 ORDER = (
-    *("a1", "b0", "x3", "x1", "x2", "x0", "g", "a1", "m", "d1", "a0", "d0", "a1", "x1", "d1", "x0",),
-    *("d0", "a0", "x3", "x1", "b1", "b0", "d1", "a0", "d0", "d1", "x0", "a0", "x1", "b1", "d1", "d0",),
-    *("a1", "x2", "x3", "x0", "b0", "d0", "a1", "b0", "d1", "x1", "x2", "a0", "b1", "a1", "x3", "x1",),
-    *("b0", "b1", "d0", "x0", "b0", "b1", "d1", "x2", "a1", "a0", "x3", "d1", "b1", "x2", "b0", "x0",),
-    *("d0", "x3", "a0", "b1", "r", "x2", "d0",),
+    *("b0", "a1", "b1", "x0", "a0", "x1", "x2", "x3", "g", "m", "d1", "a1", "x0", "d0", "d1", "a0",),
+    *("x2", "x3", "d0", "a1", "b1", "b0", "a0", "d1", "x2", "x1", "x0", "d0", "a1", "d1", "a0", "x2",),
+    *("d0", "x3", "d1", "b1", "a1", "x1", "b0", "d0", "x0", "a0", "a1", "x2", "b1", "b0", "x3", "a0",),
+    *("a1", "d1", "x1", "b0", "b1", "x2", "a0", "d0", "x0", "x3", "x1", "b0", "x0", "d1", "b1", "b0",),
+    *("d0", "x3", "d1", "b1", "x1", "r", "d0",),
 )
 
 

time: 68.3 us -> 68.8 us (level)
  no operation moved by 1% of the time
where the time goes in v4:
time: 68.8 us; the launch traced here: 68.7 us
  Pallas kernels  68.1 us (99%)
    pallas_call x1, Pallas kernels, local(): pl.pallas_call(kernel, out_shape=(f(4, 1024, 256), f(2, 1280, 128), f(2,...  65.3 us
    pallas_call x1, Pallas kernels, local(): pl.pallas_call(place, out_shape=(out(32, 512), out(32, 512), out(1024, 51...  2.78 us

profile of v4, /device:TPU:1, one launch (start us, length us, event | category | flops | bytes accessed | tf_op | source)
XLA Modules:
  0.0 68.7 jit_solution(4786154177113797616)
XLA Ops:
  0.6 65.3 %panels.1 = (f32[4,1024,256]{2,1,0:T(8,128)S(1)}, f32[2,1280,128]{2,1,0:T(8,128)S(1)}, f32[2,32,512]{2,1,0:T(8,128)S(1)}) custom-call(bf16[1024,1024]{1,0:T(8,128)(2,1)} %a_in.1, bf16[1024,512]{1,0:T(8,128)(2,1)} %r0_in.1, bf16[1024,512]{1,0:T(8,128)(2,1)} %r1_in.1, bf16[1024,512]{1,0:T(8,128)(2,1)} %k0_in.1, bf16[1024,512]{1,0:T(8,128)(2,1)} %k1_in.1, ...), custom_call_target="tpu_custom_call" | custom-call | tf_op jit(solution)/shard_map/panels/pallas_call | solution.py:377
  66.0 2.8 %place.1 = (f32[32,512]{1,0:T(8,128)}, f32[32,512]{1,0:T(8,128)}, f32[1024,512]{1,0:T(8,128)}, f32[1024,512]{1,0:T(8,128)}, f32[512,512]{1,0:T(8,128)}, /*index=5*/f32[512,512]{1,0:T(8,128)}) custom-call(f32[4,1024,256]{2,1,0:T(8,128)S(1)} %get-tuple-element.9.col, f32[2,1280,128]{2,1,0:T(8,128)S(1)} %get-tuple-element.10.d_all, ...), custom_call_target="tpu_custom_call" | custom-call | tf_op jit(solution)/shard_map/place/pallas_call | solution.py:397
